TPU v7x, 128 devices: a whole 4x4x4 slice. The times are simulated.
128 devices in a mesh: wide: 32 (over y, z, x_lo), narrow: 4 (over x_hi, core).
Axes of the slice: x: 4 (x_hi: 2, x_lo: 2; x = x_hi * 2 + x_lo), y: 4, z: 4, core: 2. Of those that a mesh axis runs over, the one named last changes fastest.
Arguments:
- target_hidden: bfloat16 [512, 16384], P(('wide', 'narrow'))
- target_weight: bfloat16 [16384, 65536], P(None, ('wide', 'narrow')), may hold values from -0.046875 to 0.046875
- draft_hidden: bfloat16 [512, 4096], P(('wide', 'narrow'))
- draft_weight: bfloat16 [4096, 65536], P(None, ('wide', 'narrow')), may hold values from -0.09375 to 0.09375
- draft_tokens: int32 [512], replicated, may hold values from 0 to 65535
Outputs:
- target_logprob: float32 [512, 65536], P(None, ('wide', 'narrow'))
- draft_logprob: float32 [512, 65536], P(None, ('wide', 'narrow'))
- residual: float32 [512, 65536], P(None, ('wide', 'narrow'))
- acceptance: float32 [512], replicated
- leftover: float32 [512], replicated
All inputs are finite; a program needn't handle non-finite values.
Results may differ from a plain program's by a relative error of at most 0.0011.
Values may be sent and summed in bfloat16 or wider, within the bound.
A program may use at most 128 MiB of HBM per device.

v0:
```python
import jax
import jax.numpy as jnp
from jax import lax
from jax.sharding import PartitionSpec as P


def on_device(target_hidden, target_weight, draft_hidden, draft_weight, draft_tokens):
    columns_dev = target_weight.shape[1]
    offset = lax.axis_index(("wide", "narrow")) * columns_dev
    target_logits = jnp.dot(
        lax.all_gather(target_hidden, ("wide", "narrow"), axis=0, tiled=True),
        target_weight,
        preferred_element_type=jnp.float32,
    )
    draft_logits = jnp.dot(
        lax.all_gather(draft_hidden, ("wide", "narrow"), axis=0, tiled=True),
        draft_weight,
        preferred_element_type=jnp.float32,
    )
    vocab_ids = offset + jnp.arange(columns_dev, dtype=jnp.int32)
    picked = draft_tokens[:, None] == vocab_ids[None, :]
    target_sel = jnp.sum(jnp.where(picked, target_logits, 0.0), axis=1)
    draft_sel = jnp.sum(jnp.where(picked, draft_logits, 0.0), axis=1)
    target_top = jnp.max(target_logits, axis=1)
    draft_top = jnp.max(draft_logits, axis=1)
    target_max, draft_max = lax.pmax((target_top, draft_top), ("wide", "narrow"))
    target_local = jnp.sum(jnp.exp(target_logits - target_max[:, None]), axis=1)
    draft_local = jnp.sum(jnp.exp(draft_logits - draft_max[:, None]), axis=1)
    target_total, draft_total, target_pick, draft_pick = lax.psum(
        (target_local, draft_local, target_sel, draft_sel), ("wide", "narrow")
    )
    target_norm = target_max + jnp.log(target_total)
    draft_norm = draft_max + jnp.log(draft_total)
    target_logprob = target_logits - target_norm[:, None]
    draft_logprob = draft_logits - draft_norm[:, None]
    excess = jnp.maximum(jnp.exp(target_logprob) - jnp.exp(draft_logprob), 0.0)
    leftover = lax.psum(jnp.sum(excess, axis=1), ("wide", "narrow"))
    residual = excess / jnp.maximum(leftover, 0.25)[:, None]
    acceptance = jnp.exp(jnp.minimum(0.0, target_pick - target_norm - (draft_pick - draft_norm)))
    return (target_logprob, draft_logprob, residual, acceptance, leftover)


def solution(mesh):
    placed = (
        P(("wide", "narrow"), None),
        P(None, ("wide", "narrow")),
        P(("wide", "narrow"), None),
        P(None, ("wide", "narrow")),
        P(),
    )
    return jax.shard_map(
        on_device,
        mesh=mesh,
        in_specs=placed,
        out_specs=(
            P(None, ("wide", "narrow")),
            P(None, ("wide", "narrow")),
            P(None, ("wide", "narrow")),
            P(),
            P(),
        ),
        check_vma=False,
    )
```

profile of v0, /device:TPU:1, one launch (start us, length us, event | category | flops | bytes accessed | tf_op | source)
XLA Modules:
  0.0 667.3 jit_solution(9454131717809929759)
XLA Ops:
  7.2 0.0 all-gather.7.cloned.1.call-start
  7.2 0.7 all-gather.7.cloned.1.call-update
  7.9 0.0 all-gather.5.cloned.1.call-start
  7.9 0.7 all-gather.5.cloned.1.call-update
  8.7 201.9 %all-gather.7.cloned.1.call-done = bf16[128,4,4096]{2,1,0:T(4,128)(2,1)} async-done(((bf16[1,4,4096]{2,1,0:T(4,128)(2,1)}), bf16[128,4,4096]{2,1,0:T(4,128)(2,1)}) %all-gather.7.cloned.1.call-update) | async-done | bytes 4194320 | tf_op jit(solution)/shard_map/all_gather | solution.py:16
  210.6 6.9 %reshape.23 = bf16[512,4096]{1,0:T(8,128)(2,1)} reshape(bf16[128,4,4096]{2,1,0:T(4,128)(2,1)} %all-gather.7.cloned.1.call-done) | data formatting | bytes 8388608
  217.5 5.9 fusion.4
  223.4 201.4 %all-gather.5.cloned.1.call-done = bf16[128,4,16384]{2,1,0:T(4,128)(2,1)} async-done(((bf16[1,4,16384]{2,1,0:T(4,128)(2,1)}), bf16[128,4,16384]{2,1,0:T(4,128)(2,1)}) %all-gather.5.cloned.1.call-update) | async-done | bytes 16777232 | tf_op jit(solution)/shard_map/all_gather | solution.py:11
  424.8 23.7 %reshape.21 = bf16[512,16384]{1,0:T(8,128)(2,1)} reshape(bf16[128,4,16384]{2,1,0:T(4,128)(2,1)} %all-gather.5.cloned.1.call-done) | data formatting | bytes 33554432
  448.5 0.0 copy-start.2
  448.5 14.9 %fusion.3 = (f32[512]{0:T(512)S(1)}, f32[512,512]{0,1:T(8,128)S(1)}) fusion(bf16[512,16384]{1,0:T(8,128)(2,1)} %reshape.21, bf16[16384,512]{1,0:T(8,128)(2,1)} %param.6), kind=kOutput, calls=%fused_computation.16 | convolution fusion | flops 8590196736 | bytes 34605056 | tf_op jit(solution)/shard_map/dot_general | solution.py:10
  463.4 0.0 copy-start
  463.4 63.5 %all-reduce.2 = (f32[512]{0:T(512)S(1)}, f32[512]{0:T(512)S(1)}) all-reduce(f32[512]{0:T(512)S(1)} %get-tuple-element.31, f32[512]{0:T(512)S(1)} %get-tuple-element.33), channel_id=1, replica_groups=mesh['wide'=32,'narrow'=4] {'wide','narrow'}, use_global_device_ids=true, to_apply=%region_1.2 | all-reduce | flops 1024 | bytes 8192 | tf_op jit(solution)/shard_map/pmax | solution.py:26
  526.9 0.0 copy-done.2
  526.9 0.5 fusion
  527.4 62.9 %all-reduce.1 = (f32[512]{0:T(512)S(1)}, f32[512]{0:T(512)S(1)}) all-reduce(f32[512]{0:T(512)S(1)} %get-tuple-element.16, f32[512]{0:T(512)S(1)} %get-tuple-element.19), channel_id=1, replica_groups=mesh['wide'=32,'narrow'=4] {'wide','narrow'}, use_global_device_ids=true, to_apply=%region_3.4 | all-reduce | flops 1024 | bytes 8192 | tf_op jit(solution)/shard_map/psum | solution.py:29
  590.2 0.0 copy-done
  590.2 1.6 fusion.2
  591.8 63.8 %all-reduce = (f32[512]{0:T(512)S(1)}, f32[512]{0:T(512)S(1)}, f32[512]{0:T(512)S(1)}) all-reduce(f32[512]{0:T(512)S(1)} %get-tuple-element.28, f32[512]{0:T(512)S(1)} %get-tuple-element.20, f32[512]{0:T(512)S(1)} %get-tuple-element.15), channel_id=1, replica_groups=mesh['wide'=32,'narrow'=4] {'wide','narrow'}, use_global_device_ids=true, to_apply=%region_9.10 | all-reduce | flops 1536 | bytes 12288 | tf_op jit(solution)/shard_map/psum | solution.py:37
  655.7 0.0 copy-start.1
  655.7 1.3 copy.13
  657.0 1.3 copy.14
  658.3 0.3 broadcast_divide_fusion
  658.6 1.3 copy.15
  659.9 0.6 minimum_exponential_fusion
  660.5 0.0 copy-done.1
  (3 shorter events, 0.0 us)
Async XLA Ops:
  7.2 203.4 %all-gather.7.cloned.1.call-start = ((), (), s32[]{:S(2)}) async-start(), calls=%async_computation.1 | async-start | bytes 4227072 | tf_op jit(solution)/shard_map/all_gather | solution.py:16
  7.9 416.9 %all-gather.5.cloned.1.call-start = ((), (), s32[]{:S(2)}) async-start(), calls=%async_computation | async-start | bytes 16908288 | tf_op jit(solution)/shard_map/all_gather | solution.py:11
  448.5 78.4 %copy-start.2 = (s32[512]{0:T(512)S(1)}, s32[512]{0:T(512)}, u32[]{:S(2)}) copy-start(s32[512]{0:T(512)} %param.9) | copy-start | bytes 6148
  463.4 126.9 %copy-start = (f32[512,512]{0,1:T(8,128)}, f32[512,512]{0,1:T(8,128)S(1)}, u32[]{:S(2)}) copy-start(f32[512,512]{0,1:T(8,128)S(1)} %get-tuple-element.32) | copy-start | bytes 3145732
  655.7 4.8 copy-start.1
Sparse Core Ops, SparseCore 0:
  9.7 200.8 all-gather.6
  212.3 212.4 all-gather.4
where the time goes:
time: 668 us; the launch traced here: 667 us
  waiting for transfers between devices  405 us (61%)
  blocking collectives  190 us (28%)
  local copies, waits for them, and re-layouts  34.5 us (5%)
  matrix products  20.8 us (3%)
  between operations  14.1 us (2%)
    all_gather x1, waiting for transfers between devices, on_device(): lax.all_gather(draft_hidden, ('wide', 'narrow'), axis=0, tiled=True)  202 us
    all_gather x1, waiting for transfers between devices, on_device(): lax.all_gather(target_hidden, ('wide', 'narrow'), axis=0, tiled=True)  201 us
    psum x1, blocking collectives, on_device(): leftover = lax.psum(jnp.sum(excess, axis=1), ('wide', 'narrow'))  63.8 us
    pmax x1, blocking collectives, on_device(): lax.pmax((target_top, draft_top), ('wide', 'narrow'))  63.5 us
    psum x1, blocking collectives, on_device(): lax.psum((target_local, draft_local, target_sel, draft_sel), ('wide', 'na...  62.9 us
    unnamed x11, local copies, waits for them, and re-layouts  34.5 us
    dot_general x1, matrix products, on_device(): jnp.dot(lax.all_gather(target_hidden, ('wide', 'narrow'), axis=0, tiled=T...  14.9 us
  transfers between devices with their start and end apart: 2, of which 2 were waited for; matrix products, arithmetic and copies ran while one was open for 2% of the time, Pallas kernels for 0%

commit v1 on v0

--- a/solution.py
+++ b/solution.py
@@ -34,7 +34,7 @@
     target_logprob = target_logits - target_norm[:, None]
     draft_logprob = draft_logits - draft_norm[:, None]
     excess = jnp.maximum(jnp.exp(target_logprob) - jnp.exp(draft_logprob), 0.0)
-    leftover = lax.psum(jnp.sum(excess, axis=1), ("wide", "narrow"))
+    leftover = jnp.sum(lax.all_gather(jnp.sum(excess, axis=1), ("wide", "narrow")), axis=0)
     residual = excess / jnp.maximum(leftover, 0.25)[:, None]
     acceptance = jnp.exp(jnp.minimum(0.0, target_pick - target_norm - (draft_pick - draft_norm)))
     return (target_logprob, draft_logprob, residual, acceptance, leftover)

time: 668 us -> 779 us (1.17)
  blocking collectives: 190 us -> 302 us
    all_gather x0 -> x1, blocking collectives: none -> 174 us  [on_device(): lax.all_gather(jnp.sum(excess, axis=1), ('wide', 'narrow'))]
    psum x1 -> x0, blocking collectives: 63.8 us -> none  [on_device(): leftover = lax.psum(jnp.sum(excess, axis=1), ('wide', 'narrow'))]
where the time goes in v1:
time: 779 us; the launch traced here: 778 us
  waiting for transfers between devices  404 us (52%)
  blocking collectives  302 us (39%)
  local copies, waits for them, and re-layouts  34.5 us (4%)
  matrix products  20.8 us (3%)
  between operations  14.1 us (2%)
    all_gather x1, waiting for transfers between devices, on_device(): lax.all_gather(draft_hidden, ('wide', 'narrow'), axis=0, tiled=True)  202 us
    all_gather x1, waiting for transfers between devices, on_device(): lax.all_gather(target_hidden, ('wide', 'narrow'), axis=0, tiled=True)  201 us
    all_gather x1, blocking collectives, on_device(): lax.all_gather(jnp.sum(excess, axis=1), ('wide', 'narrow'))  174 us
    pmax x1, blocking collectives, on_device(): lax.pmax((target_top, draft_top), ('wide', 'narrow'))  64.1 us
    psum x1, blocking collectives, on_device(): lax.psum((target_local, draft_local, target_sel, draft_sel), ('wide', 'na...  63.1 us
    unnamed x11, local copies, waits for them, and re-layouts  34.5 us
  transfers between devices with their start and end apart: 2, of which 2 were waited for; matrix products, arithmetic and copies ran while one was open for 2% of the time, Pallas kernels for 0%

profile of v1, /device:TPU:1, one launch (start us, length us, event | category | flops | bytes accessed | tf_op | source)
XLA Modules:
  0.0 778.4 jit_solution(16490339980075460253)
XLA Ops:
  7.2 0.0 all-gather.9.cloned.1.call-start
  7.2 0.7 all-gather.9.cloned.1.call-update
  7.9 0.0 all-gather.7.cloned.1.call-start
  7.9 0.7 all-gather.7.cloned.1.call-update
  8.7 201.9 %all-gather.9.cloned.1.call-done = bf16[128,4,4096]{2,1,0:T(4,128)(2,1)} async-done(((bf16[1,4,4096]{2,1,0:T(4,128)(2,1)}), bf16[128,4,4096]{2,1,0:T(4,128)(2,1)}) %all-gather.9.cloned.1.call-update) | async-done | bytes 4194320 | tf_op jit(solution)/shard_map/all_gather | solution.py:16
  210.6 6.9 reshape.26
  217.5 5.9 fusion.4
  223.4 200.9 %all-gather.7.cloned.1.call-done = bf16[128,4,16384]{2,1,0:T(4,128)(2,1)} async-done(((bf16[1,4,16384]{2,1,0:T(4,128)(2,1)}), bf16[128,4,16384]{2,1,0:T(4,128)(2,1)}) %all-gather.7.cloned.1.call-update) | async-done | bytes 16777232 | tf_op jit(solution)/shard_map/all_gather | solution.py:11
  424.3 23.7 %reshape.24 = bf16[512,16384]{1,0:T(8,128)(2,1)} reshape(bf16[128,4,16384]{2,1,0:T(4,128)(2,1)} %all-gather.7.cloned.1.call-done) | data formatting | bytes 33554432
  448.0 0.0 copy-start.2
  448.0 14.9 %fusion.3 = (f32[512]{0:T(512)S(1)}, f32[512,512]{0,1:T(8,128)S(1)}) fusion(bf16[512,16384]{1,0:T(8,128)(2,1)} %reshape.24, bf16[16384,512]{1,0:T(8,128)(2,1)} %param.6), kind=kOutput, calls=%fused_computation.16 | convolution fusion | flops 8590196736 | bytes 34605056 | tf_op jit(solution)/shard_map/dot_general | solution.py:10
  462.9 0.0 copy-start
  462.9 64.1 %all-reduce.1 = (f32[512]{0:T(512)S(1)}, f32[512]{0:T(512)S(1)}) all-reduce(f32[512]{0:T(512)S(1)} %get-tuple-element.33, f32[512]{0:T(512)S(1)} %get-tuple-element.35), channel_id=1, replica_groups=mesh['wide'=32,'narrow'=4] {'wide','narrow'}, use_global_device_ids=true, to_apply=%region_1.2 | all-reduce | flops 1024 | bytes 8192 | tf_op jit(solution)/shard_map/pmax | solution.py:26
  527.0 0.0 copy-done.2
  527.0 0.5 fusion
  527.5 63.1 %all-reduce = (f32[512]{0:T(512)S(1)}, f32[512]{0:T(512)S(1)}, f32[512]{0:T(512)S(1)}, f32[512]{0:T(512)S(1)}) all-reduce(f32[512]{0:T(512)S(1)} %get-tuple-element.16, f32[512]{0:T(512)S(1)} %get-tuple-element.19, f32[512]{0:T(512)S(1)} %get-tuple-element.20, ...), channel_id=1, replica_groups=mesh['wide'=32,'narrow'=4] {'wide','narrow'}, use_global_device_ids=true, to_apply=%region_3.4 | all-reduce | flops 2048 | bytes 16384 | tf_op jit(solution)/shard_map/psum | solution.py:29
  590.6 0.6 minimum_exponential_fusion
  591.1 0.0 copy-done
  591.2 1.6 fusion.2
  592.7 174.3 %all-gather.3 = f32[128,1,512]{2,1,0:T(1,128)S(1)} all-gather(f32[1,1,512]{2,1,0:T(1,128)S(1)} %bitcast.9), channel_id=2, replica_groups=mesh['wide'=32,'narrow'=4] {'wide','narrow'}, dimensions={0}, use_global_device_ids=true | all-gather | bytes 264192 | tf_op jit(solution)/shard_map/all_gather | solution.py:37
  767.1 0.2 reduce_sum.57
  767.3 0.0 copy-start.1
  767.3 1.3 copy.13
  768.6 1.3 copy.14
  769.9 0.3 broadcast_divide_fusion
  770.2 1.3 copy.15
  771.5 0.0 copy-done.1
  (2 shorter events, 0.0 us)
Async XLA Ops:
  7.2 203.4 %all-gather.9.cloned.1.call-start = ((), (), s32[]{:S(2)}) async-start(), calls=%async_computation.1 | async-start | bytes 4227072 | tf_op jit(solution)/shard_map/all_gather | solution.py:16
  7.9 416.4 %all-gather.7.cloned.1.call-start = ((), (), s32[]{:S(2)}) async-start(), calls=%async_computation | async-start | bytes 16908288 | tf_op jit(solution)/shard_map/all_gather | solution.py:11
  448.0 79.0 %copy-start.2 = (s32[512]{0:T(512)S(1)}, s32[512]{0:T(512)}, u32[]{:S(2)}) copy-start(s32[512]{0:T(512)} %param.9) | copy-start | bytes 6148
  462.9 128.3 %copy-start = (f32[512,512]{0,1:T(8,128)}, f32[512,512]{0,1:T(8,128)S(1)}, u32[]{:S(2)}) copy-start(f32[512,512]{0,1:T(8,128)S(1)} %get-tuple-element.34) | copy-start | bytes 3145732
  767.3 4.2 copy-start.1
Sparse Core Ops, SparseCore 0:
  9.7 200.8 all-gather.8
  212.3 211.9 all-gather.6

commit v2 on v0

--- a/solution.py
+++ b/solution.py
@@ -13,7 +13,15 @@
         preferred_element_type=jnp.float32,
     )
     draft_logits = jnp.dot(
-        lax.all_gather(draft_hidden, ("wide", "narrow"), axis=0, tiled=True),
+        jnp.concatenate(
+            lax.all_to_all(
+                jnp.stack([draft_hidden] * lax.axis_size(("wide", "narrow"))),
+                ("wide", "narrow"),
+                0,
+                0,
+            ),
+            axis=0,
+        ),
         draft_weight,
         preferred_element_type=jnp.float32,
     )

time: 668 us -> 510 us (0.76)
  waiting for transfers between devices: 405 us -> 228 us
  starting transfers between devices: 0.08 us -> 12 us
    all_gather x1 -> x0, waiting for transfers between devices: 202 us -> none  [on_device(): lax.all_gather(draft_hidden, ('wide', 'narrow'), axis=0, tiled=True)]
    all_to_all x0 -> x1, waiting for transfers between devices: none -> 59.1 us  [on_device(): lax.all_to_all(jnp.stack([draft_hidden] * lax.axis_size(('wide', 'narrow'...]
    all_gather x1, waiting for transfers between devices: 201 us -> 168 us  [on_device(): lax.all_gather(target_hidden, ('wide', 'narrow'), axis=0, tiled=True)]
    all_to_all x0 -> x1, starting transfers between devices: none -> 12 us  [on_device(): lax.all_to_all(jnp.stack([draft_hidden] * lax.axis_size(('wide', 'narrow'...]
    reshape x0 -> x1, local copies, waits for them, and re-layouts: none -> 6.98 us  [on_device(): jnp.concatenate(lax.all_to_all(jnp.stack([draft_hidden] * lax.axis_size((...]
    unnamed x11 -> x10, local copies, waits for them, and re-layouts: 34.5 us -> 27.6 us
  transfers between devices with their start and end apart: 2 -> 2, of which waited for: 2 -> 2; matrix products, arithmetic and copies ran while one was open for 2% -> 3% of each run, Pallas kernels for 0% -> 0%
where the time goes in v2:
time: 510 us; the launch traced here: 508 us
  waiting for transfers between devices  228 us (45%)
  blocking collectives  191 us (37%)
  local copies, waits for them, and re-layouts  39.4 us (8%)
  matrix products  20.8 us (4%)
  between operations  14.1 us (3%)
  starting transfers between devices  12 us (2%)
    all_gather x1, waiting for transfers between devices, on_device(): lax.all_gather(target_hidden, ('wide', 'narrow'), axis=0, tiled=True)  168 us
    pmax x1, blocking collectives, on_device(): lax.pmax((target_top, draft_top), ('wide', 'narrow'))  64.4 us
    psum x1, blocking collectives, on_device(): leftover = lax.psum(jnp.sum(excess, axis=1), ('wide', 'narrow'))  64.3 us
    psum x1, blocking collectives, on_device(): lax.psum((target_local, draft_local, target_sel, draft_sel), ('wide', 'na...  62.5 us
    all_to_all x1, waiting for transfers between devices, on_device(): lax.all_to_all(jnp.stack([draft_hidden] * lax.axis_size(('wide', 'narrow'...  59.1 us
    unnamed x10, local copies, waits for them, and re-layouts  27.6 us
    dot_general x1, matrix products, on_device(): jnp.dot(lax.all_gather(target_hidden, ('wide', 'narrow'), axis=0, tiled=T...  14.9 us
    all_to_all x1, starting transfers between devices, on_device(): lax.all_to_all(jnp.stack([draft_hidden] * lax.axis_size(('wide', 'narrow'...  12 us
  transfers between devices with their start and end apart: 2, of which 2 were waited for; matrix products, arithmetic and copies ran while one was open for 3% of the time, Pallas kernels for 0%

profile of v2, /device:TPU:1, one launch (start us, length us, event | category | flops | bytes accessed | tf_op | source)
XLA Modules:
  0.0 508.4 jit_solution(8402078956621744996)
XLA Ops:
  7.2 0.0 all-gather.3.cloned.1.call-start
  7.2 0.7 all-gather.3.cloned.1.call-update
  7.9 4.8 stack.2
  12.7 12.0 %all-to-all-start = ((bf16[128,4,4096]{2,1,0:T(4,128)(2,1)}), bf16[128,4,4096]{2,1,0:T(4,128)(2,1)}, u32[]{:S(2)}, u32[]{:S(2)}) async-start(bf16[128,4,4096]{2,1,0:T(4,128)(2,1)} %stack.2), calls=%async_computation | async-start | bytes 8388608 | tf_op jit(solution)/shard_map/all_to_all | solution.py:17
  24.7 59.1 %all-to-all-done = bf16[128,4,4096]{2,1,0:T(4,128)(2,1)} async-done(((bf16[128,4,4096]{2,1,0:T(4,128)(2,1)}), bf16[128,4,4096]{2,1,0:T(4,128)(2,1)}, u32[]{:S(2)}, u32[]{:S(2)}) %all-to-all-start) | async-done | bytes 4194336 | tf_op jit(solution)/shard_map/all_to_all | solution.py:17
  83.8 7.0 %reshape.25 = bf16[512,4096]{1,0:T(8,128)(2,1)} reshape(bf16[128,4,4096]{2,1,0:T(4,128)(2,1)} %all-to-all-done) | data formatting | bytes 8388608 | tf_op jit(solution)/shard_map/reshape | solution.py:16
  90.8 5.9 %fusion.4 = (f32[512]{0:T(512)S(1)}, f32[512,512]{0,1:T(8,128)S(1)}) fusion(bf16[512,4096]{1,0:T(8,128)(2,1)} %reshape.25, bf16[4096,512]{1,0:T(8,128)(2,1)} %param.8), kind=kOutput, calls=%fused_computation.17 | convolution fusion | flops 2147745280 | bytes 9439232 | tf_op jit(solution)/shard_map/dot_general | solution.py:15
  96.7 168.2 %all-gather.3.cloned.1.call-done = bf16[128,4,16384]{2,1,0:T(4,128)(2,1)} async-done(((bf16[1,4,16384]{2,1,0:T(4,128)(2,1)}), bf16[128,4,16384]{2,1,0:T(4,128)(2,1)}) %all-gather.3.cloned.1.call-update) | async-done | bytes 16777232 | tf_op jit(solution)/shard_map/all_gather | solution.py:11
  264.9 23.7 %reshape.27 = bf16[512,16384]{1,0:T(8,128)(2,1)} reshape(bf16[128,4,16384]{2,1,0:T(4,128)(2,1)} %all-gather.3.cloned.1.call-done) | data formatting | bytes 33554432
  288.6 0.0 copy-start.2
  288.6 14.9 %fusion.3 = (f32[512]{0:T(512)S(1)}, f32[512,512]{0,1:T(8,128)S(1)}) fusion(bf16[512,16384]{1,0:T(8,128)(2,1)} %reshape.27, bf16[16384,512]{1,0:T(8,128)(2,1)} %param.6), kind=kOutput, calls=%fused_computation.16 | convolution fusion | flops 8590196736 | bytes 34605056 | tf_op jit(solution)/shard_map/dot_general | solution.py:10
  303.4 0.0 copy-start
  303.5 64.4 %all-reduce.2 = (f32[512]{0:T(512)S(1)}, f32[512]{0:T(512)S(1)}) all-reduce(f32[512]{0:T(512)S(1)} %get-tuple-element.31, f32[512]{0:T(512)S(1)} %get-tuple-element.33), channel_id=1, replica_groups=mesh['wide'=32,'narrow'=4] {'wide','narrow'}, use_global_device_ids=true, to_apply=%region_1.2 | all-reduce | flops 1024 | bytes 8192 | tf_op jit(solution)/shard_map/pmax | solution.py:34
  367.8 0.0 copy-done.2
  367.8 0.5 fusion
  368.3 62.5 %all-reduce.1 = (f32[512]{0:T(512)S(1)}, f32[512]{0:T(512)S(1)}) all-reduce(f32[512]{0:T(512)S(1)} %get-tuple-element.16, f32[512]{0:T(512)S(1)} %get-tuple-element.19), channel_id=1, replica_groups=mesh['wide'=32,'narrow'=4] {'wide','narrow'}, use_global_device_ids=true, to_apply=%region_3.4 | all-reduce | flops 1024 | bytes 8192 | tf_op jit(solution)/shard_map/psum | solution.py:37
  430.9 0.0 copy-done
  430.9 1.6 fusion.2
  432.4 64.3 %all-reduce = (f32[512]{0:T(512)S(1)}, f32[512]{0:T(512)S(1)}, f32[512]{0:T(512)S(1)}) all-reduce(f32[512]{0:T(512)S(1)} %get-tuple-element.28, f32[512]{0:T(512)S(1)} %get-tuple-element.20, f32[512]{0:T(512)S(1)} %get-tuple-element.15), channel_id=1, replica_groups=mesh['wide'=32,'narrow'=4] {'wide','narrow'}, use_global_device_ids=true, to_apply=%region_9.10 | all-reduce | flops 1536 | bytes 12288 | tf_op jit(solution)/shard_map/psum | solution.py:45
  496.8 0.0 copy-start.1
  496.8 1.3 copy.13
  498.1 1.3 copy.14
  499.4 0.3 broadcast_divide_fusion
  499.7 1.3 copy.15
  501.0 0.0 copy-done.1
  501.0 0.6 minimum_exponential_fusion
  (3 shorter events, 0.0 us)
Async XLA Ops:
  7.2 257.7 %all-gather.3.cloned.1.call-start = ((), (), s32[]{:S(2)}) async-start(), calls=%async_computation.1 | async-start | bytes 16908288 | tf_op jit(solution)/shard_map/all_gather | solution.py:11
  12.7 71.1 %all-to-all-start = ((bf16[128,4,4096]{2,1,0:T(4,128)(2,1)}), bf16[128,4,4096]{2,1,0:T(4,128)(2,1)}, u32[]{:S(2)}, u32[]{:S(2)}) async-start(bf16[128,4,4096]{2,1,0:T(4,128)(2,1)} %stack.2), calls=%async_computation | async-start | bytes 8388608 | tf_op jit(solution)/shard_map/all_to_all | solution.py:17
  288.6 79.3 %copy-start.2 = (s32[512]{0:T(512)S(1)}, s32[512]{0:T(512)}, u32[]{:S(2)}) copy-start(s32[512]{0:T(512)} %param.9) | copy-start | bytes 6148
  303.4 127.4 %copy-start = (f32[512,512]{0,1:T(8,128)}, f32[512,512]{0,1:T(8,128)S(1)}, u32[]{:S(2)}) copy-start(f32[512,512]{0,1:T(8,128)S(1)} %get-tuple-element.32) | copy-start | bytes 3145732
  496.8 4.2 copy-start.1
Sparse Core Ops, SparseCore 0:
  9.7 255.1 all-gather.2
